TPU v7x, 32 devices: a whole 2x2x4 slice. The times are simulated.
32 devices in a mesh: groups: 2 (over y), ep: 8 (over z, core), rep: 2 (over x).
Axes of the slice: x: 2, y: 2, z: 4, core: 2. Of those that a mesh axis runs over, the one named last changes fastest.
Arguments:
- tokens: bfloat16 [1024, 2048], P(('groups', 'ep')), parts along dimension 0, may hold values from -6 to 6
- choices: int32 [1024, 8], P(('groups', 'ep')), parts along dimension 0, may hold values from 0 to 15, all different within a row; in each aligned block of 64 rows (0 to 63, 64 to 127, ...) at most 64 rows name the same one
- route_weight: float32 [1024, 8], P(('groups', 'ep')), parts along dimension 0, may hold values from 0.05 to 0.3
- gate_proj: bfloat16 [16, 2048, 768], P('ep', None, 'rep'), may hold values from -0.125 to 0.125
- up_proj: bfloat16 [16, 2048, 768], P('ep', None, 'rep'), may hold values from -0.125 to 0.125
- down_proj: bfloat16 [16, 768, 2048], P('ep', 'rep'), may hold values from -0.21875 to 0.21875
Outputs:
- mixed: bfloat16 [1024, 2048], P(('groups', 'ep'), 'rep'), parts along dimension 0
There are 2 independent parts, one for each index of `groups`. A program takes and returns all parts, laid end to end along the dimension named above; an argument that names none is the same for every part. Nothing has to cross between parts.
Inputs may be any that keep to these rules, and one draw needn't show every extreme that they name: `choices`: each row names 8 different experts. In each aligned block of 64 rows no expert is named by more than 64 rows, a bound that some block reaches.
All inputs are finite; a program needn't handle non-finite values.
Results may differ from a plain program's by a relative error of at most 0.0085.
Values may be sent and summed in bfloat16 or wider, within the bound.
A program may use at most 64 MiB of HBM per device.

v0:
```python
import jax
import jax.numpy as jnp
from jax import lax
from jax.sharding import PartitionSpec as P


def local(tokens, choices, route_weight, gate_proj, up_proj, down_proj):
    n_ep = lax.axis_size("ep")
    n_rep = lax.axis_size("rep")
    exp_dev = gate_proj.shape[0]
    num_experts = exp_dev * n_ep
    tok_rows = tokens.shape[0]
    picks = choices.shape[1]
    width = tokens.shape[1]
    slot_cap = min(tok_rows, (2 * tok_rows * picks // num_experts + n_rep - 1) // n_rep * n_rep)
    slot_total = num_experts * slot_cap
    flat_choice = choices.reshape(-1)
    expert_ids = jnp.arange(num_experts, dtype=jnp.int32)
    onehot = (flat_choice[:, None] == expert_ids[None, :]).astype(jnp.int32)
    before = jnp.cumsum(onehot, axis=0) - onehot
    rank = jnp.sum(before * onehot, axis=1)
    slot_ids = flat_choice * slot_cap + rank
    all_slots = jnp.arange(slot_total, dtype=jnp.int32)
    select = (slot_ids[:, None] == all_slots[None, :]).reshape(tok_rows, picks, slot_total)
    dispatch = jnp.sum(select.astype(jnp.bfloat16), axis=1)
    combine = jnp.sum(jnp.where(select, route_weight[:, :, None], 0.0), axis=1)
    combine_high = combine.astype(jnp.bfloat16)
    combine_low = (combine - combine_high.astype(jnp.float32)).astype(jnp.bfloat16)
    buffer = jnp.einsum("ts,td->sd", dispatch, tokens, preferred_element_type=jnp.float32)
    buffer = buffer.astype(jnp.bfloat16).reshape(n_ep, exp_dev, slot_cap, width)
    arrived = lax.all_to_all(buffer, "ep", split_axis=0, concat_axis=0, tiled=True)
    gate_val = jnp.einsum("sjcd,jdh->sjch", arrived, gate_proj, preferred_element_type=jnp.float32)
    up_val = jnp.einsum("sjcd,jdh->sjch", arrived, up_proj, preferred_element_type=jnp.float32)
    hidden = (jax.nn.silu(gate_val) * up_val).astype(jnp.bfloat16)
    partial_out = jnp.einsum(
        "sjch,jhd->sjcd", hidden, down_proj, preferred_element_type=jnp.float32
    )
    expert_out = lax.psum_scatter(
        partial_out.astype(jnp.bfloat16), "rep", scatter_dimension=3, tiled=True
    )
    returned = lax.all_to_all(expert_out, "ep", split_axis=0, concat_axis=0, tiled=True)
    returned_rows = returned.reshape(slot_total, -1)
    mixed = jnp.dot(combine_high, returned_rows, preferred_element_type=jnp.float32)
    mixed = mixed + jnp.dot(combine_low, returned_rows, preferred_element_type=jnp.float32)
    return mixed.astype(jnp.bfloat16)


def solution(mesh):
    placed = (
        P(("groups", "ep"), None),
        P(("groups", "ep"), None),
        P(("groups", "ep"), None),
        P("ep", None, "rep"),
        P("ep", None, "rep"),
        P("ep", "rep", None),
    )
    return jax.shard_map(
        local, mesh=mesh, in_specs=placed, out_specs=P(("groups", "ep"), "rep"), check_vma=False
    )
```

profile of v0, /device:TPU:0, one launch (start us, length us, event | category | flops | bytes accessed | tf_op | source)
XLA Modules:
  0.0 249.3 jit_solution(14430175307891705766)
XLA Ops:
  6.5 0.9 copy.36
  7.5 0.1 eq.43
  7.6 0.1 eq.39
  7.7 1.2 reduce-window.6
  8.8 0.2 slice_reduce_fusion
  9.1 0.1 fusion.28
  9.2 0.1 reduce_sum.33
  9.3 0.1 copy.39
  9.3 0.7 multiply_add_fusion
  10.0 0.1 copy.40
  10.1 0.7 fusion.21
  10.8 2.2 convolution_convert_fusion
  13.1 100.4 %all_to_all.10 = bf16[8,2,64,2048]{3,2,1,0:T(8,128)(2,1)S(1)} all-to-all(bf16[8,2,64,2048]{3,2,1,0:T(8,128)(2,1)S(1)} %bitcast.67), channel_id=1, replica_groups=mesh['groups'=2,'ep'=8,'rep'=2] {'ep'}, dimensions={0} | all-to-all | bytes 8388608 | tf_op jit(solution)/shard_map/all_to_all | solution.py:31
  113.5 2.0 copy-done.1
  115.4 3.6 %fusion.2 = f32[2,8,64,384]{3,2,1,0:T(8,128)} fusion(bf16[8,2,64,2048]{3,2,1,0:T(8,128)(2,1)S(1)} %all_to_all.10, bf16[2,2048,384]{2,1,0:T(8,128)(2,1)S(1)} %copy-done.3), kind=kOutput, calls=%fused_computation.4 | convolution fusion | flops 1610612736 | bytes 8912896 | tf_op jit(solution)/shard_map/sjcd,jdh->sjch/dot_general | solution.py:32
  119.0 8.2 %convert_bitcast_fusion = bf16[8,2,64,2048]{3,2,0,1:T(8,128)(2,1)} fusion(bf16[2,384,2048]{2,1,0:T(8,128)(2,1)S(1)} %copy-done, f32[2,8,64,384]{3,2,1,0:T(8,128)} %fusion.2, bf16[2,2048,384]{2,1,0:T(8,128)(2,1)} %param.10, bf16[8,2,64,2048]{3,2,1,0:T(8,128)(2,1)} %copy-done.1), kind=kOutput, calls=%fused_computation | convolution fusion | flops 3225681920 | bytes 16252928 | tf_op jit(solution)/shard_map/sjch,jhd->sjcd/dot_general | solution.py:35
  127.3 53.3 %reduce-scatter.2.cloned.1.call-done = bf16[8,2,64,1024]{3,2,0,1:T(8,128)(2,1)} async-done(((bf16[8,2,64,2048]{3,2,0,1:T(8,128)(2,1)}), bf16[8,2,64,1024]{3,2,0,1:T(8,128)(2,1)}) %reduce-scatter.2.cloned.1.call-update) | async-done | bytes 2097168 | tf_op jit(solution)/shard_map/reduce_scatter | solution.py:38
  180.6 3.2 %copy.44 = bf16[8,2,64,1024]{3,2,1,0:T(8,128)(2,1)} copy(bf16[8,2,64,1024]{3,2,0,1:T(8,128)(2,1)} %reduce-scatter.2.cloned.1.call-done) | data formatting | bytes 4194304 | tf_op jit(solution)/shard_map/reduce_scatter | solution.py:38
  183.8 4.7 %all-to-all-start.1 = ((bf16[8,2,64,1024]{3,2,1,0:T(8,128)(2,1)}), bf16[8,2,64,1024]{3,2,1,0:T(8,128)(2,1)}, u32[]{:S(2)}, u32[]{:S(2)}) async-start(bf16[8,2,64,1024]{3,2,1,0:T(8,128)(2,1)} %copy.44), calls=%async_computation.2 | async-start | bytes 4194304 | tf_op jit(solution)/shard_map/all_to_all | solution.py:41
  188.5 0.1 copy.41
  188.6 0.7 select_reduce_fusion
  189.3 48.4 %all-to-all-done.1 = bf16[8,2,64,1024]{3,2,1,0:T(8,128)(2,1)} async-done(((bf16[8,2,64,1024]{3,2,1,0:T(8,128)(2,1)}), bf16[8,2,64,1024]{3,2,1,0:T(8,128)(2,1)}, u32[]{:S(2)}, u32[]{:S(2)}) %all-to-all-start.1) | async-done | bytes 2097184 | tf_op jit(solution)/shard_map/all_to_all | solution.py:41
  237.7 2.1 fusion.24
  239.8 2.7 %fusion.20 = bf16[64,1024]{1,0:T(8,128)(2,1)} fusion(f32[64,1024]{1,0:T(8,128)S(1)} %fusion.24, bf16[1024,1024]{1,0:T(8,128)(2,1)} %bitcast.11, f32[64,1024]{1,0:T(8,128)S(1)} %select_reduce_fusion), kind=kOutput, calls=%fused_computation.20 | convolution fusion | flops 134610944 | bytes 2752512 | tf_op jit(solution)/shard_map/dot_general | solution.py:44
  (12 shorter events, 0.1 us)
Async XLA Ops:
  6.5 112.5 %copy-start = (bf16[2,384,2048]{2,1,0:T(8,128)(2,1)S(1)}, bf16[2,384,2048]{2,1,0:T(8,128)(2,1)}, u32[]{:S(2)}) copy-start(bf16[2,384,2048]{2,1,0:T(8,128)(2,1)} %param.11) | copy-start | bytes 9437188
  6.5 174.1 %reduce-scatter.2.cloned.1.call-start = ((), (), s32[]{:S(2)}) async-start(), calls=%async_computation.3 | async-start | bytes 6291456 | tf_op jit(solution)/shard_map/reduce_scatter | solution.py:38
  13.0 102.4 %copy-start.3 = (bf16[2,2048,384]{2,1,0:T(8,128)(2,1)S(1)}, bf16[2,2048,384]{2,1,0:T(8,128)(2,1)}, u32[]{:S(2)}) copy-start(bf16[2,2048,384]{2,1,0:T(8,128)(2,1)} %param.9) | copy-start | bytes 9437188
  113.5 2.0 copy-start.1
  183.8 4.8 %copy-start.2 = (f32[64,8]{0,1:T(8,128)S(1)}, f32[64,8]{0,1:T(8,128)}, u32[]{:S(2)}) copy-start(f32[64,8]{0,1:T(8,128)} %param.8) | copy-start | bytes 6148
  183.8 53.9 %all-to-all-start.1 = ((bf16[8,2,64,1024]{3,2,1,0:T(8,128)(2,1)}), bf16[8,2,64,1024]{3,2,1,0:T(8,128)(2,1)}, u32[]{:S(2)}, u32[]{:S(2)}) async-start(bf16[8,2,64,1024]{3,2,1,0:T(8,128)(2,1)} %copy.44), calls=%async_computation.2 | async-start | bytes 4194304 | tf_op jit(solution)/shard_map/all_to_all | solution.py:41
Sparse Core Ops, SparseCore 0:
  127.4 53.1 reduce-scatter.1
where the time goes:
time: 250 us; the launch traced here: 249 us
  waiting for transfers between devices  102 us (41%)
  blocking collectives  100 us (40%)
  matrix products  18.8 us (8%)
  between operations  13.5 us (5%)
  local copies, waits for them, and re-layouts  6.8 us (3%)
  starting transfers between devices  4.75 us (2%)
  other arithmetic  3.39 us (1%)
    all_to_all x1, blocking collectives, local(): lax.all_to_all(buffer, 'ep', split_axis=0, concat_axis=0, tiled=True)  100 us
    reduce_scatter x1, waiting for transfers between devices, local(): lax.psum_scatter(partial_out.astype(jnp.bfloat16), 'rep', scatter_dimensi...  53.3 us
    all_to_all x1, waiting for transfers between devices, local(): lax.all_to_all(expert_out, 'ep', split_axis=0, concat_axis=0, tiled=True)  48.4 us
    dot_general x1, matrix products, local(): jnp.einsum('sjch,jhd->sjcd', hidden, down_proj, preferred_element_type=jn...  8.24 us
  transfers between devices with their start and end apart: 2, of which 2 were waited for; matrix products, arithmetic and copies ran while one was open for 0% of the time, Pallas kernels for 0%

commit v1 on v0

v1 whole, which is shorter than its diff:
```python
import functools

import jax
import jax.numpy as jnp
from jax import lax
from jax.experimental import pallas as pl
from jax.experimental.pallas import tpu as pltpu
from jax.sharding import PartitionSpec as P

MESH = pl.DeviceIdType.MESH
BF16 = jnp.bfloat16
F32 = jnp.float32
LANES = 128
N_Z = 4
AG_Z, AG_X, AG_OWN, AG_C, RS_C, RS_X, RS_Z, N_SEM = 0, 4, 8, 9, 17, 21, 25, 29


def partner(z, k):
    return (z, z + 1 - 2 * lax.rem(z, 2), lax.rem(z + 2, 4), 3 - z)[k]


def kernel(
    tokens, choices, route, gate, up, down, out,
    xg, gv, uv, dv, own, c_send, c_recv, x_send, x_recv, z_send, z_recv, acc,
    local_sem, send_sem, recv_sem,
):
    e = lax.axis_index("ep")
    x = lax.axis_index("rep")
    z, c = e // 2, lax.rem(e, 2)
    rows, half = tokens.shape[0], tokens.shape[1] // 2
    pieces = xg.shape[-1]

    weights = []
    for i, (a, b) in enumerate(((gate, gv), (up, uv), (down, dv))):
        for j in range(2):
            weights.append(pltpu.make_async_copy(a.at[j], b.at[j], local_sem.at[2 * i + j]))
    loads = [
        pltpu.make_async_copy(
            tokens.at[:, pl.ds(h * half, half)], xg.at[e, h, :, pl.ds(0, half)], local_sem.at[6 + h]
        )
        for h in range(2)
    ]
    for copy in loads + weights:
        copy.start()

    core_peer, x_peer = {"ep": 2 * z + 1 - c}, {"rep": 1 - x}
    z_peer = [{"ep": 2 * partner(z, k) + c} for k in range(N_Z)]
    barrier = pltpu.get_barrier_semaphore()
    peers = [core_peer, x_peer] + z_peer[1:]
    for peer in peers:
        pl.semaphore_signal(barrier, inc=1, device_id=peer, device_id_type=MESH)

    lane = lax.broadcasted_iota(jnp.int32, (rows, LANES), 1)
    dense = jnp.zeros((rows, LANES), F32)
    for k in range(choices.shape[1]):
        dense = dense + jnp.where(lane == choices[:, k : k + 1], route[:, k : k + 1], 0.0)
    high = dense.astype(BF16)
    xg[e, 0, :, half:pieces] = high
    xg[e, 1, :, half:pieces] = (dense - high.astype(F32)).astype(BF16)
    for copy in loads:
        copy.wait()
    pl.semaphore_wait(barrier, len(peers))

    started = []

    def send(src, dst, slot, peer):
        copy = pltpu.make_async_remote_copy(
            src_ref=src, dst_ref=dst, send_sem=send_sem.at[slot], recv_sem=recv_sem.at[slot],
            device_id=peer, device_id_type=MESH,
        )
        copy.start()
        started.append(copy)

    def arrive(dst, slot, peer):
        pltpu.make_async_remote_copy(
            src_ref=dst, dst_ref=dst, send_sem=send_sem.at[slot], recv_sem=recv_sem.at[slot],
            device_id=peer, device_id_type=MESH,
        ).wait_recv()

    def block(k, core):
        return 2 * partner(z, k) + core

    def gather_z(k):
        piece = xg.at[block(k, c), x]
        arrive(piece, AG_Z + k, z_peer[k])
        send(piece, piece, AG_X + k, x_peer)
        send(piece, piece, AG_C + 2 * k, core_peer)

    def gather_x(k):
        piece = xg.at[block(k, c), 1 - x]
        arrive(piece, AG_X + k, x_peer)
        send(piece, piece, AG_C + 2 * k + 1, core_peer)

    def gather_c(k):
        if k == 0:
            arrive(xg.at[block(0, 1 - c)], AG_OWN, core_peer)
        else:
            arrive(xg.at[block(k, 1 - c), x], AG_C + 2 * k, core_peer)
            arrive(xg.at[block(k, 1 - c), 1 - x], AG_C + 2 * k + 1, core_peer)

    mine = c == 0

    def compute(k):
        at = pl.ds(2 * partner(z, k), 2)
        tok = [xg[at, h, :, 0:half].reshape(2 * rows, half) for h in range(2)]
        w = [xg[at, h, :, half:pieces].reshape(2 * rows, LANES).astype(F32) for h in range(2)]
        w = w[0] + w[1]
        lanes = lax.broadcasted_iota(jnp.int32, w.shape, 1)
        hidden = []
        for j in range(2):
            g, u = (
                jnp.dot(tok[0], ref[j, 0:half], preferred_element_type=F32)
                + jnp.dot(tok[1], ref[j, half : 2 * half], preferred_element_type=F32)
                for ref in (gv, uv)
            )
            weight = jnp.sum(jnp.where(lanes == 2 * e + j, w, 0.0), axis=1, keepdims=True)
            hidden.append((g / (1.0 + jnp.exp(-g)) * u * weight).astype(BF16))
        for h in range(2):
            cols = slice(h * half, (h + 1) * half)
            p = jnp.dot(hidden[0], dv[0, :, cols], preferred_element_type=F32)
            p = p + jnp.dot(hidden[1], dv[1, :, cols], preferred_element_type=F32)
            own[k, h] = jnp.where(mine, p[:rows], p[rows:])
            c_send[k, h] = jnp.where(mine, p[rows:], p[:rows]).astype(BF16)
        send(c_send.at[k], c_recv.at[k], RS_C + k, core_peer)

    def reduce_c(k):
        arrive(c_recv.at[k], RS_C + k, core_peer)
        x_send[k] = (own[k, 1 - x] + c_recv[k, 1 - x].astype(F32)).astype(BF16)
        send(x_send.at[k], x_recv.at[k], RS_X + k, x_peer)

    def reduce_x(k):
        arrive(x_recv.at[k], RS_X + k, x_peer)
        total = own[k, x] + c_recv[k, x].astype(F32) + x_recv[k].astype(F32)
        if k == 0:
            acc[...] = total
        else:
            z_send[k] = total.astype(BF16)
            send(z_send.at[k], z_recv.at[k], RS_Z + k, z_peer[k])

    for k in range(1, N_Z):
        send(xg.at[e, x], xg.at[e, x], AG_Z + k, z_peer[k])
    send(xg.at[e], xg.at[e], AG_OWN, core_peer)

    gather_z(1)
    gather_c(0)
    for copy in weights:
        copy.wait()
    compute(0)
    gather_x(1)
    gather_z(2)
    gather_c(1)
    compute(1)
    reduce_c(0)
    gather_x(2)
    gather_z(3)
    gather_c(2)
    compute(2)
    reduce_c(1)
    reduce_x(0)
    gather_x(3)
    gather_c(3)
    compute(3)
    reduce_c(2)
    reduce_x(1)
    reduce_c(3)
    reduce_x(2)
    reduce_x(3)
    total = acc[...]
    for k in range(1, N_Z):
        arrive(z_recv.at[k], RS_Z + k, z_peer[k])
        total = total + z_recv[k].astype(F32)
    out[...] = total.astype(BF16)
    for copy in started:
        copy.wait_send()


def fused(tokens, choices, route_weight, gate_proj, up_proj, down_proj):
    n_ep = lax.axis_size("ep")
    rows, width = tokens.shape
    half, piece = width // 2, (rows, width // 2)
    anywhere, vmem = pl.BlockSpec(memory_space=pl.ANY), pl.BlockSpec(memory_space=pltpu.VMEM)
    return pl.pallas_call(
        kernel,
        out_shape=jax.ShapeDtypeStruct(piece, BF16),
        in_specs=[anywhere, vmem, vmem, anywhere, anywhere, anywhere],
        out_specs=vmem,
        scratch_shapes=[
            pltpu.VMEM((n_ep, 2, rows, half + LANES), BF16),
            pltpu.VMEM(gate_proj.shape, BF16),
            pltpu.VMEM(up_proj.shape, BF16),
            pltpu.VMEM(down_proj.shape, BF16),
            pltpu.VMEM((N_Z, 2) + piece, F32),
            pltpu.VMEM((N_Z, 2) + piece, BF16),
            pltpu.VMEM((N_Z, 2) + piece, BF16),
            pltpu.VMEM((N_Z,) + piece, BF16),
            pltpu.VMEM((N_Z,) + piece, BF16),
            pltpu.VMEM((N_Z,) + piece, BF16),
            pltpu.VMEM((N_Z,) + piece, BF16),
            pltpu.VMEM(piece, F32),
            pltpu.SemaphoreType.DMA((8,)),
            pltpu.SemaphoreType.DMA((N_SEM,)),
            pltpu.SemaphoreType.DMA((N_SEM,)),
        ],
        compiler_params=pltpu.CompilerParams(
            collective_id=0, has_side_effects=True, vmem_limit_bytes=56 * 2**20
        ),
    )(tokens, choices, route_weight, gate_proj, up_proj, down_proj)


def slotted(tokens, choices, route_weight, gate_proj, up_proj, down_proj):
    n_ep = lax.axis_size("ep")
    n_rep = lax.axis_size("rep")
    exp_dev = gate_proj.shape[0]
    num_experts = exp_dev * n_ep
    tok_rows, width = tokens.shape
    picks = choices.shape[1]
    slot_cap = min(tok_rows, (2 * tok_rows * picks // num_experts + n_rep - 1) // n_rep * n_rep)
    slot_total = num_experts * slot_cap
    flat_choice = choices.reshape(-1)
    onehot = flat_choice[:, None] == jnp.arange(num_experts, dtype=jnp.int32)[None, :]
    order = jnp.arange(flat_choice.shape[0])
    earlier = (order[None, :] < order[:, None]).astype(BF16)
    before = jnp.dot(earlier, onehot.astype(BF16), preferred_element_type=F32)
    rank = jnp.sum(jnp.where(onehot, before, 0.0), axis=1).astype(jnp.int32)
    slot_ids = flat_choice * slot_cap + rank
    all_slots = jnp.arange(slot_total, dtype=jnp.int32)
    select = (slot_ids[:, None] == all_slots[None, :]).reshape(tok_rows, picks, slot_total)
    dispatch = jnp.sum(select.astype(BF16), axis=1)
    combine = jnp.sum(jnp.where(select, route_weight[:, :, None], 0.0), axis=1)
    high = combine.astype(BF16)
    low = (combine - high.astype(F32)).astype(BF16)
    buffer = jnp.einsum("ts,td->sd", dispatch, tokens, preferred_element_type=F32)
    buffer = buffer.astype(BF16).reshape(n_ep, exp_dev, slot_cap, width)
    arrived = lax.all_to_all(buffer, "ep", split_axis=0, concat_axis=0, tiled=True)
    gate_val = jnp.einsum("sjcd,jdh->sjch", arrived, gate_proj, preferred_element_type=F32)
    up_val = jnp.einsum("sjcd,jdh->sjch", arrived, up_proj, preferred_element_type=F32)
    hidden = (jax.nn.silu(gate_val) * up_val).astype(BF16)
    partial_out = jnp.einsum("sjch,jhd->sjcd", hidden, down_proj, preferred_element_type=F32)
    expert_out = lax.psum_scatter(
        partial_out.astype(BF16), "rep", scatter_dimension=3, tiled=True
    )
    returned = lax.all_to_all(expert_out, "ep", split_axis=0, concat_axis=0, tiled=True)
    returned = returned.reshape(slot_total, -1)
    mixed = jnp.dot(high, returned, preferred_element_type=F32)
    mixed = mixed + jnp.dot(low, returned, preferred_element_type=F32)
    return mixed.astype(BF16)


def solution(mesh):
    small = mesh.shape["ep"] == 2 * N_Z and mesh.shape["rep"] == 2
    placed = (
        P(("groups", "ep"), None),
        P(("groups", "ep"), None),
        P(("groups", "ep"), None),
        P("ep", None, "rep"),
        P("ep", None, "rep"),
        P("ep", "rep", None),
    )
    return jax.shard_map(
        fused if small else slotted,
        mesh=mesh,
        in_specs=placed,
        out_specs=P(("groups", "ep"), "rep"),
        check_vma=False,
    )
```

time: 250 us -> 51.6 us (0.21)
  waiting for transfers between devices: 102 us -> 0 us
  blocking collectives: 100 us -> 0 us
  Pallas kernels: 0 us -> 46.3 us
  matrix products: 18.8 us -> 0 us
  between operations: 13.5 us -> 0.01 us
  starting transfers between devices: 4.75 us -> 0 us
  other arithmetic: 3.39 us -> 0 us
    all_to_all x1 -> x0, blocking collectives: 100 us -> none  [local(): lax.all_to_all(buffer, 'ep', split_axis=0, concat_axis=0, tiled=True)]
    reduce_scatter x1 -> x0, waiting for transfers between devices: 53.3 us -> none  [local(): lax.psum_scatter(partial_out.astype(jnp.bfloat16), 'rep', scatter_dimensi...]
    all_to_all x1 -> x0, waiting for transfers between devices: 48.4 us -> none  [local(): lax.all_to_all(expert_out, 'ep', split_axis=0, concat_axis=0, tiled=True)]
    pallas_call x0 -> x1, Pallas kernels: none -> 46.3 us  [fused(): pl.pallas_call(kernel, out_shape=jax.ShapeDtypeStruct(piece, BF16), in_sp...]
    dot_general x5 -> x0, matrix products: 18.8 us -> none  [the longest x1 8.24 us: local(): jnp.einsum('sjch,jhd->sjcd', hidden, down_proj, preferred_element_type=jn...]
    all_to_all x1 -> x0, starting transfers between devices: 4.75 us -> none  [local(): lax.all_to_all(expert_out, 'ep', split_axis=0, concat_axis=0, tiled=True)]
    reduce_scatter x1 -> x0, local copies, waits for them, and re-layouts: 3.17 us -> none  [local(): lax.psum_scatter(partial_out.astype(jnp.bfloat16), 'rep', scatter_dimensi...]
  transfers between devices with their start and end apart: 2 -> 0, of which waited for: 2 -> 0; matrix products, arithmetic and copies ran while one was open for 0% -> 0% of each run, Pallas kernels for 0% -> 0%
where the time goes in v1:
time: 51.6 us; the launch traced here: 50.6 us
  Pallas kernels  46.3 us (90%)
  local copies, waits for them, and re-layouts  4.32 us (8%)
    pallas_call x1, Pallas kernels, fused(): pl.pallas_call(kernel, out_shape=jax.ShapeDtypeStruct(piece, BF16), in_sp...  46.3 us
    unnamed x3, local copies, waits for them, and re-layouts  4.32 us

profile of v1, /device:TPU:0, one launch (start us, length us, event | category | flops | bytes accessed | tf_op | source)
XLA Modules:
  0.0 50.6 jit_solution(8802009114399824327)
XLA Ops:
  0.0 1.4 %copy.7.choices = s32[64,8]{1,0:T(8,128)} copy(s32[64,8]{0,1:T(8,128)} %param.7) | data formatting | bytes 4096 | tf_op args[1]
  1.4 1.4 %copy.8.route = f32[64,8]{1,0:T(8,128)} copy(f32[64,8]{0,1:T(8,128)} %param.8) | data formatting | bytes 4096 | tf_op args[2]
  2.8 46.3 %shard_map.64 = bf16[64,1024]{1,0:T(8,128)(2,1)} custom-call(bf16[64,2048]{1,0:T(8,128)(2,1)} %tokens.1, s32[64,8]{1,0:T(8,128)} %copy.7.choices, f32[64,8]{1,0:T(8,128)} %copy.8.route, bf16[2,2048,384]{2,1,0:T(8,128)(2,1)} %gate.1, bf16[2,2048,384]{2,1,0:T(8,128)(2,1)} %up.1, bf16[2,384,2048]{2,1,0:T(8,128)(2,1)} %down.1), custom_call_target="tpu_custom_call" | custom-call | tf_op jit(solution)/shard_map/pallas_call | solution.py:182
  49.0 1.6 %copy.10 = bf16[64,1024]{1,0:T(8,128)(2,1)} copy(bf16[64,1024]{1,0:T(8,128)(2,1)} %shard_map.64) | data formatting | bytes 262144

commit v2 on v1

--- a/solution.py
+++ b/solution.py
@@ -12,11 +12,12 @@
 F32 = jnp.float32
 LANES = 128
 N_Z = 4
-AG_Z, AG_X, AG_OWN, AG_C, RS_C, RS_X, RS_Z, N_SEM = 0, 4, 8, 9, 17, 21, 25, 29
-
-
-def partner(z, k):
-    return (z, z + 1 - 2 * lax.rem(z, 2), lax.rem(z + 2, 4), 3 - z)[k]
+AG_Z, AG_X, AG_OWN, AG_C, RS_C, RS_X, RS_Z, FORWARD, N_SEM = 0, 4, 8, 9, 17, 21, 25, 29, 37
+
+
+def source(z, k):
+    first, last = (3 - z) // 3, z // 3
+    return (z, z - 1 + 2 * first, z + 1 + first - 3 * last, 3 * (1 - z // 2))[k]
 
 
 def kernel(
@@ -44,45 +45,61 @@
         copy.start()
 
     core_peer, x_peer = {"ep": 2 * z + 1 - c}, {"rep": 1 - x}
-    z_peer = [{"ep": 2 * partner(z, k) + c} for k in range(N_Z)]
+    z_peer = [{"ep": 2 * source(z, k) + c} for k in range(N_Z)]
+    right, left = {"ep": 2 * lax.rem(z + 1, N_Z) + c}, {"ep": 2 * lax.rem(z + 3, N_Z) + c}
     barrier = pltpu.get_barrier_semaphore()
     peers = [core_peer, x_peer] + z_peer[1:]
     for peer in peers:
         pl.semaphore_signal(barrier, inc=1, device_id=peer, device_id_type=MESH)
 
-    lane = lax.broadcasted_iota(jnp.int32, (rows, LANES), 1)
-    dense = jnp.zeros((rows, LANES), F32)
-    for k in range(choices.shape[1]):
-        dense = dense + jnp.where(lane == choices[:, k : k + 1], route[:, k : k + 1], 0.0)
+    experts = 2 * lax.axis_size("ep")
+    index = lax.broadcasted_iota(jnp.int32, (experts, rows), 0)
+    dense = jnp.zeros((experts, rows), F32)
+    for k in range(choices.shape[0]):
+        dense = dense + jnp.where(index == choices[k : k + 1, :], route[k : k + 1, :], 0.0)
     high = dense.astype(BF16)
-    xg[e, 0, :, half:pieces] = high
-    xg[e, 1, :, half:pieces] = (dense - high.astype(F32)).astype(BF16)
+    unit = lax.broadcasted_iota(jnp.int32, (experts, LANES), 0)
+    unit = (unit == lax.broadcasted_iota(jnp.int32, (experts, LANES), 1)).astype(BF16)
+    for h, part in enumerate((high, (dense - high.astype(F32)).astype(BF16))):
+        turned = lax.dot_general(
+            part, unit, (((0,), (0,)), ((), ())), preferred_element_type=F32
+        )
+        xg[e, h, :, half:pieces] = turned.astype(BF16)
     for copy in loads:
         copy.wait()
     pl.semaphore_wait(barrier, len(peers))
 
     started = []
 
-    def send(src, dst, slot, peer):
-        copy = pltpu.make_async_remote_copy(
-            src_ref=src, dst_ref=dst, send_sem=send_sem.at[slot], recv_sem=recv_sem.at[slot],
+    def remote(src, dst, out_slot, in_slot, peer):
+        return pltpu.make_async_remote_copy(
+            src_ref=src, dst_ref=dst, send_sem=send_sem.at[out_slot], recv_sem=recv_sem.at[in_slot],
             device_id=peer, device_id_type=MESH,
         )
-        copy.start()
-        started.append(copy)
+
+    def send(src, dst, slot, peer, in_slot=None, when=None):
+        copy = remote(src, dst, slot, slot if in_slot is None else in_slot, peer)
+        started.append((copy, when))
+        if when is None:
+            copy.start()
+        else:
+            pl.when(when)(copy.start)
 
     def arrive(dst, slot, peer):
-        pltpu.make_async_remote_copy(
-            src_ref=dst, dst_ref=dst, send_sem=send_sem.at[slot], recv_sem=recv_sem.at[slot],
-            device_id=peer, device_id_type=MESH,
-        ).wait_recv()
+        remote(dst, dst, slot, slot, peer).wait_recv()
 
     def block(k, core):
-        return 2 * partner(z, k) + core
+        return 2 * source(z, k) + core
 
     def gather_z(k):
+        src = source(z, k)
         piece = xg.at[block(k, c), x]
-        arrive(piece, AG_Z + k, z_peer[k])
+        arrive(piece, AG_Z + src, z_peer[k])
+        slot = FORWARD + 2 * k
+        if k != 2:
+            send(piece, piece, slot, right, AG_Z + src, jnp.logical_and(src < z, z < N_Z - 1))
+        if k != 1:
+            send(piece, piece, slot + 1, left, AG_Z + src, jnp.logical_and(src > z, z > 0))
         send(piece, piece, AG_X + k, x_peer)
         send(piece, piece, AG_C + 2 * k, core_peer)
 
@@ -101,7 +118,7 @@
     mine = c == 0
 
     def compute(k):
-        at = pl.ds(2 * partner(z, k), 2)
+        at = pl.ds(2 * source(z, k), 2)
         tok = [xg[at, h, :, 0:half].reshape(2 * rows, half) for h in range(2)]
         w = [xg[at, h, :, half:pieces].reshape(2 * rows, LANES).astype(F32) for h in range(2)]
         w = w[0] + w[1]
@@ -135,10 +152,10 @@
             acc[...] = total
         else:
             z_send[k] = total.astype(BF16)
-            send(z_send.at[k], z_recv.at[k], RS_Z + k, z_peer[k])
-
-    for k in range(1, N_Z):
-        send(xg.at[e, x], xg.at[e, x], AG_Z + k, z_peer[k])
+            send(z_send.at[k], z_recv.at[z], RS_Z + k, z_peer[k], RS_Z + z)
+
+    send(xg.at[e, x], xg.at[e, x], FORWARD, right, AG_Z + z, z < N_Z - 1)
+    send(xg.at[e, x], xg.at[e, x], FORWARD + 1, left, AG_Z + z, z > 0)
     send(xg.at[e], xg.at[e], AG_OWN, core_peer)
 
     gather_z(1)
@@ -146,32 +163,36 @@
     for copy in weights:
         copy.wait()
     compute(0)
+    gather_z(2)
     gather_x(1)
-    gather_z(2)
+    gather_z(3)
+    reduce_c(0)
     gather_c(1)
     compute(1)
-    reduce_c(0)
     gather_x(2)
-    gather_z(3)
+    reduce_c(1)
     gather_c(2)
     compute(2)
-    reduce_c(1)
+    gather_x(3)
+    reduce_c(2)
     reduce_x(0)
-    gather_x(3)
     gather_c(3)
     compute(3)
-    reduce_c(2)
     reduce_x(1)
     reduce_c(3)
     reduce_x(2)
     reduce_x(3)
     total = acc[...]
     for k in range(1, N_Z):
-        arrive(z_recv.at[k], RS_Z + k, z_peer[k])
-        total = total + z_recv[k].astype(F32)
+        src = source(z, k)
+        arrive(z_recv.at[src], RS_Z + src, z_peer[k])
+        total = total + z_recv[src].astype(F32)
     out[...] = total.astype(BF16)
-    for copy in started:
-        copy.wait_send()
+    for copy, when in started:
+        if when is None:
+            copy.wait_send()
+        else:
+            pl.when(when)(copy.wait_send)
 
 
 def fused(tokens, choices, route_weight, gate_proj, up_proj, down_proj):
@@ -204,7 +225,7 @@
         compiler_params=pltpu.CompilerParams(
             collective_id=0, has_side_effects=True, vmem_limit_bytes=56 * 2**20
         ),
-    )(tokens, choices, route_weight, gate_proj, up_proj, down_proj)
+    )(tokens, choices.T, route_weight.T, gate_proj, up_proj, down_proj)
 
 
 def slotted(tokens, choices, route_weight, gate_proj, up_proj, down_proj):

time: 51.6 us -> 45.3 us (0.88); the launches traced: 50.6 us -> 45.1 us
  Pallas kernels: 46.3 us -> 43.5 us
  local copies, waits for them, and re-layouts: 4.32 us -> 1.57 us
    pallas_call x1, Pallas kernels: 46.3 us -> 43.5 us  [fused(): pl.pallas_call(kernel, out_shape=jax.ShapeDtypeStruct(piece, BF16), in_sp...]
    unnamed x3 -> x1, local copies, waits for them, and re-layouts: 4.32 us -> 1.57 us
where the time goes in v2:
time: 45.3 us; the launch traced here: 45.1 us
  Pallas kernels  43.5 us (96%)
  local copies, waits for them, and re-layouts  1.57 us (3%)
    pallas_call x1, Pallas kernels, fused(): pl.pallas_call(kernel, out_shape=jax.ShapeDtypeStruct(piece, BF16), in_sp...  43.5 us
    unnamed x1, local copies, waits for them, and re-layouts  1.57 us

profile of v2, /device:TPU:0, one launch (start us, length us, event | category | flops | bytes accessed | tf_op | source)
XLA Modules:
  0.0 45.1 jit_solution(11478563587563984546)
XLA Ops:
  0.0 43.5 %shard_map.64 = bf16[64,1024]{1,0:T(8,128)(2,1)} custom-call(bf16[64,2048]{1,0:T(8,128)(2,1)} %tokens.1, s32[8,64]{1,0:T(8,128)} %bitcast.2, f32[8,64]{1,0:T(8,128)} %bitcast.3, bf16[2,2048,384]{2,1,0:T(8,128)(2,1)} %gate.1, bf16[2,2048,384]{2,1,0:T(8,128)(2,1)} %up.1, bf16[2,384,2048]{2,1,0:T(8,128)(2,1)} %down.1), custom_call_target="tpu_custom_call" | custom-call | tf_op jit(solution)/shard_map/pallas_call | solution.py:203
  43.5 1.6 %copy.8 = bf16[64,1024]{1,0:T(8,128)(2,1)} copy(bf16[64,1024]{1,0:T(8,128)(2,1)} %shard_map.64) | data formatting | bytes 262144

commit v3 on v2

--- a/solution.py
+++ b/solution.py
@@ -12,6 +12,7 @@
 F32 = jnp.float32
 LANES = 128
 N_Z = 4
+PARTS = 2
 AG_Z, AG_X, AG_OWN, AG_C, RS_C, RS_X, RS_Z, FORWARD, N_SEM = 0, 4, 8, 9, 17, 21, 25, 29, 37
 
 
@@ -71,49 +72,56 @@
 
     started = []
 
-    def remote(src, dst, out_slot, in_slot, peer):
+    def remote(src, dst, out_slot, in_slot, peer, r):
         return pltpu.make_async_remote_copy(
-            src_ref=src, dst_ref=dst, send_sem=send_sem.at[out_slot], recv_sem=recv_sem.at[in_slot],
+            src_ref=src, dst_ref=dst, send_sem=send_sem.at[out_slot, r], recv_sem=recv_sem.at[in_slot, r],
             device_id=peer, device_id_type=MESH,
         )
 
-    def send(src, dst, slot, peer, in_slot=None, when=None):
-        copy = remote(src, dst, slot, slot if in_slot is None else in_slot, peer)
+    def send(src, dst, slot, peer, in_slot=None, when=None, r=0):
+        copy = remote(src, dst, slot, slot if in_slot is None else in_slot, peer, r)
         started.append((copy, when))
         if when is None:
             copy.start()
         else:
             pl.when(when)(copy.start)
 
-    def arrive(dst, slot, peer):
-        remote(dst, dst, slot, slot, peer).wait_recv()
+    def arrive(dst, slot, peer, r=0):
+        remote(dst, dst, slot, slot, peer, r).wait_recv()
+
+    def cut(r):
+        return pl.ds(r * (rows // PARTS), rows // PARTS)
 
     def block(k, core):
         return 2 * source(z, k) + core
 
     def gather_z(k):
-        src = source(z, k)
-        piece = xg.at[block(k, c), x]
-        arrive(piece, AG_Z + src, z_peer[k])
-        slot = FORWARD + 2 * k
-        if k != 2:
-            send(piece, piece, slot, right, AG_Z + src, jnp.logical_and(src < z, z < N_Z - 1))
-        if k != 1:
-            send(piece, piece, slot + 1, left, AG_Z + src, jnp.logical_and(src > z, z > 0))
-        send(piece, piece, AG_X + k, x_peer)
-        send(piece, piece, AG_C + 2 * k, core_peer)
+        src, slot = source(z, k), FORWARD + 2 * k
+        for r in range(PARTS):
+            piece = xg.at[block(k, c), x, cut(r)]
+            arrive(piece, AG_Z + src, z_peer[k], r)
+            if k != 2:
+                on = jnp.logical_and(src < z, z < N_Z - 1)
+                send(piece, piece, slot, right, AG_Z + src, on, r)
+            if k != 1:
+                on = jnp.logical_and(src > z, z > 0)
+                send(piece, piece, slot + 1, left, AG_Z + src, on, r)
+            send(piece, piece, AG_X + k, x_peer, r=r)
+            send(piece, piece, AG_C + 2 * k, core_peer, r=r)
 
     def gather_x(k):
-        piece = xg.at[block(k, c), 1 - x]
-        arrive(piece, AG_X + k, x_peer)
-        send(piece, piece, AG_C + 2 * k + 1, core_peer)
+        for r in range(PARTS):
+            piece = xg.at[block(k, c), 1 - x, cut(r)]
+            arrive(piece, AG_X + k, x_peer, r)
+            send(piece, piece, AG_C + 2 * k + 1, core_peer, r=r)
 
     def gather_c(k):
         if k == 0:
             arrive(xg.at[block(0, 1 - c)], AG_OWN, core_peer)
-        else:
-            arrive(xg.at[block(k, 1 - c), x], AG_C + 2 * k, core_peer)
-            arrive(xg.at[block(k, 1 - c), 1 - x], AG_C + 2 * k + 1, core_peer)
+            return
+        for r in range(PARTS):
+            arrive(xg.at[block(k, 1 - c), x, cut(r)], AG_C + 2 * k, core_peer, r)
+            arrive(xg.at[block(k, 1 - c), 1 - x, cut(r)], AG_C + 2 * k + 1, core_peer, r)
 
     mine = c == 0
 
@@ -142,20 +150,26 @@
 
     def reduce_c(k):
         arrive(c_recv.at[k], RS_C + k, core_peer)
-        x_send[k] = (own[k, 1 - x] + c_recv[k, 1 - x].astype(F32)).astype(BF16)
-        send(x_send.at[k], x_recv.at[k], RS_X + k, x_peer)
+        for r in range(PARTS):
+            at = cut(r)
+            x_send[k, at] = (own[k, 1 - x, at] + c_recv[k, 1 - x, at].astype(F32)).astype(BF16)
+            send(x_send.at[k, at], x_recv.at[k, at], RS_X + k, x_peer, r=r)
 
     def reduce_x(k):
-        arrive(x_recv.at[k], RS_X + k, x_peer)
-        total = own[k, x] + c_recv[k, x].astype(F32) + x_recv[k].astype(F32)
-        if k == 0:
-            acc[...] = total
-        else:
-            z_send[k] = total.astype(BF16)
-            send(z_send.at[k], z_recv.at[z], RS_Z + k, z_peer[k], RS_Z + z)
-
-    send(xg.at[e, x], xg.at[e, x], FORWARD, right, AG_Z + z, z < N_Z - 1)
-    send(xg.at[e, x], xg.at[e, x], FORWARD + 1, left, AG_Z + z, z > 0)
+        for r in range(PARTS):
+            at = cut(r)
+            arrive(x_recv.at[k, at], RS_X + k, x_peer, r)
+            total = own[k, x, at] + c_recv[k, x, at].astype(F32) + x_recv[k, at].astype(F32)
+            if k == 0:
+                acc[at] = total
+            else:
+                z_send[k, at] = total.astype(BF16)
+                send(z_send.at[k, at], z_recv.at[z, at], RS_Z + k, z_peer[k], RS_Z + z, r=r)
+
+    for r in range(PARTS):
+        piece = xg.at[e, x, cut(r)]
+        send(piece, piece, FORWARD, right, AG_Z + z, z < N_Z - 1, r)
+        send(piece, piece, FORWARD + 1, left, AG_Z + z, z > 0, r)
     send(xg.at[e], xg.at[e], AG_OWN, core_peer)
 
     gather_z(1)
@@ -182,12 +196,14 @@
     reduce_c(3)
     reduce_x(2)
     reduce_x(3)
-    total = acc[...]
-    for k in range(1, N_Z):
-        src = source(z, k)
-        arrive(z_recv.at[src], RS_Z + src, z_peer[k])
-        total = total + z_recv[src].astype(F32)
-    out[...] = total.astype(BF16)
+    for r in range(PARTS):
+        at = cut(r)
+        total = acc[at]
+        for k in range(1, N_Z):
+            src = source(z, k)
+            arrive(z_recv.at[src, at], RS_Z + src, z_peer[k], r)
+            total = total + z_recv[src, at].astype(F32)
+        out[at] = total.astype(BF16)
     for copy, when in started:
         if when is None:
             copy.wait_send()
@@ -219,8 +235,8 @@
             pltpu.VMEM((N_Z,) + piece, BF16),
             pltpu.VMEM(piece, F32),
             pltpu.SemaphoreType.DMA((8,)),
-            pltpu.SemaphoreType.DMA((N_SEM,)),
-            pltpu.SemaphoreType.DMA((N_SEM,)),
+            pltpu.SemaphoreType.DMA((N_SEM, PARTS)),
+            pltpu.SemaphoreType.DMA((N_SEM, PARTS)),
         ],
         compiler_params=pltpu.CompilerParams(
             collective_id=0, has_side_effects=True, vmem_limit_bytes=56 * 2**20

time: 45.3 us -> 44.4 us (0.980)
  Pallas kernels: 43.5 us -> 42.6 us
    pallas_call x1, Pallas kernels: 43.5 us -> 42.6 us  [fused(): pl.pallas_call(kernel, out_shape=jax.ShapeDtypeStruct(piece, BF16), in_sp...]
where the time goes in v3:
time: 44.4 us; the launch traced here: 44.2 us
  Pallas kernels  42.6 us (96%)
  local copies, waits for them, and re-layouts  1.57 us (4%)
    pallas_call x1, Pallas kernels, fused(): pl.pallas_call(kernel, out_shape=jax.ShapeDtypeStruct(piece, BF16), in_sp...  42.6 us
    unnamed x1, local copies, waits for them, and re-layouts  1.57 us

profile of v3, /device:TPU:0, one launch (start us, length us, event | category | flops | bytes accessed | tf_op | source)
XLA Modules:
  0.0 44.2 jit_solution(10751638870745425228)
XLA Ops:
  0.0 42.6 %shard_map.64 = bf16[64,1024]{1,0:T(8,128)(2,1)} custom-call(bf16[64,2048]{1,0:T(8,128)(2,1)} %tokens.1, s32[8,64]{1,0:T(8,128)} %bitcast.2, f32[8,64]{1,0:T(8,128)} %bitcast.3, bf16[2,2048,384]{2,1,0:T(8,128)(2,1)} %gate.1, bf16[2,2048,384]{2,1,0:T(8,128)(2,1)} %up.1, bf16[2,384,2048]{2,1,0:T(8,128)(2,1)} %down.1), custom_call_target="tpu_custom_call" | custom-call | tf_op jit(solution)/shard_map/pallas_call | solution.py:219
  42.6 1.6 %copy.8 = bf16[64,1024]{1,0:T(8,128)(2,1)} copy(bf16[64,1024]{1,0:T(8,128)(2,1)} %shard_map.64) | data formatting | bytes 262144
